TPU v7x, 32 devices: a whole 2x2x4 slice. The times are simulated.
32 devices in a mesh: group: 2 (over y), tile: 8 (over z, x), lev: 2 (over core).
Axes of the slice: x: 2, y: 2, z: 4, core: 2. Of those that a mesh axis runs over, the one named last changes fastest.
Arguments:
- members_x: bfloat16 [80, 32, 32768], P(None, 'lev', ('group', 'tile')), parts along dimension 2, may hold values from -6 to 6
- error_early: bfloat16 [32, 32768], P('lev', ('group', 'tile')), parts along dimension 1, may hold values from -6 to 6
- error_late: bfloat16 [32, 32768], P('lev', ('group', 'tile')), parts along dimension 1, may hold values from -6 to 6
- energy: bfloat16 [32, 32768], P('lev', ('group', 'tile')), parts along dimension 1, may hold values from 0.29882812 to 3
- vert_weight: float32 [8, 32], replicated, may hold values from 0.05 to 1
- tile_lists: int32 [16, 2, 3], P(('group', 'tile')), parts along dimension 0, may hold values from 0 to 7, as said below
- obs_block: int32 [16, 4096], P(('group', 'tile')), parts along dimension 0, may hold values from 0 to 1, never falling along the last dimension, each value on 1 to 4095 neighbouring positions
- obs_bin: int32 [16, 4096], P(('group', 'tile')), parts along dimension 0, may hold values from 0 to 7
- obs_column: int32 [16, 4096], P(('group', 'tile')), parts along dimension 0, may hold values from 0 to 2047
- obs_pert: bfloat16 [16, 80, 4096], P(('group', 'tile')), parts along dimension 0, may hold values from -6 to 6
- innovation: float32 [16, 4096], P(('group', 'tile')), parts along dimension 0, may hold values from -6 to 6
- inv_variance: float32 [16, 4096], P(('group', 'tile')), parts along dimension 0, may hold values from 0.25 to 4
- horiz_weight: float32 [16, 4, 4096], P(('group', 'tile')), parts along dimension 0, may hold values from 0.1 to 1
Outputs:
- impact: float32 [16, 2048, 2], P(('group', 'tile'), None, 'lev'), parts along dimension 0
There are 2 independent parts, one for each index of `group`. A program takes and returns all parts, laid end to end along the dimension named above; an argument that names none is the same for every part. Nothing has to cross between parts.
Inputs may be any that keep to these rules, and one draw needn't show every extreme that they name: `tile_lists`: in each row, the 2 * (3) entries are distinct tiles and none is the row's own tile. `obs_block`: within a row block numbers never fall; every block of a row holds 1 to 4095 observations.
All inputs are finite; a program needn't handle non-finite values.
Results may differ from a plain program's by a relative error of at most 0.0029.
Values may be sent and summed in bfloat16 or wider, within the bound.
A program may use at most 64 MiB of HBM per device.

v0:
```python
import functools

import jax
import jax.numpy as jnp
from jax import lax
from jax.experimental import pallas as pl
from jax.experimental.pallas import tpu as pltpu
from jax.sharding import PartitionSpec as P

CHUNK = 256
LANES = 128
VMEM_LIMIT = 56 * 1024 * 1024


def split_high_low(values):
    high = values.astype(jnp.bfloat16)
    low = (values - high.astype(jnp.float32)).astype(jnp.bfloat16)
    return high, low


def ring_tile(place, peers):
    if peers % 2:
        return place
    return jnp.where(place < peers // 2, 2 * place, 2 * (peers - 1 - place) + 1)


def ring_place(tile, peers):
    if peers % 2:
        return tile
    return jnp.where(tile % 2 == 0, tile // 2, peers - 1 - tile // 2)


def remote(src, dst, send_sem, recv_sem, target):
    return pltpu.make_async_remote_copy(
        src_ref=src,
        dst_ref=dst,
        send_sem=send_sem,
        recv_sem=recv_sem,
        device_id=target,
        device_id_type=pl.DeviceIdType.MESH,
    )


def greet(peers, tile, lev):
    barrier = pltpu.get_barrier_semaphore()
    for offset in range(1, peers):
        pl.semaphore_signal(
            barrier,
            inc=1,
            device_id={"tile": lax.rem(tile + offset, peers)},
            device_id_type=pl.DeviceIdType.MESH,
        )
    pl.semaphore_signal(
        barrier, inc=1, device_id={"lev": 1 - lev}, device_id_type=pl.DeviceIdType.MESH
    )
    pl.semaphore_wait(barrier, peers)


def exchange_kernel(
    peers,
    group,
    members_ref,
    early_ref,
    late_ref,
    energy_ref,
    weight_ref,
    packed_ref,
    pert_ref,
    summary_ref,
    lookups_ref,
    perts_ref,
    members_buf,
    own_buf,
    sent_buf,
    other_buf,
    table_buf,
    in_sem,
    out_sem,
    lev_send,
    lev_recv,
    look_send,
    look_recv,
    ring_send,
    ring_recv,
    local_sem,
):
    tile = lax.axis_index("tile")
    lev = lax.axis_index("lev")
    chunks, members, levels, width = members_buf.shape
    bins = own_buf.shape[1]
    share = perts_ref.shape[2]
    piece = share // 2
    place = ring_place(tile, peers)
    half = pl.multiple_of(lev * share, LANES)
    partner = {"lev": 1 - lev}

    def fetch(chunk):
        here = pl.ds(pl.multiple_of(chunk * width, LANES), width)
        return pltpu.make_async_copy(members_ref.at[:, :, here], members_buf.at[chunk], in_sem.at[chunk])

    for chunk in range(chunks):
        fetch(chunk).start()
    own_look = pltpu.make_async_copy(packed_ref, lookups_ref.at[tile], local_sem.at[0])
    own_look.start()
    own_pert = pltpu.make_async_copy(
        pert_ref.at[0, :, pl.ds(half, share)], perts_ref.at[tile], local_sem.at[1]
    )
    own_pert.start()
    greet(peers, tile, lev)

    look_copies = []
    for offset in range(1, peers):
        copy = remote(
            packed_ref,
            lookups_ref.at[tile],
            look_send.at[offset - 1],
            look_recv.at[offset - 1],
            {"tile": lax.rem(tile + offset, peers)},
        )
        copy.start()
        look_copies.append(copy)

    steps = peers // 2

    def ring_copy(way, step, part):
        towards = 1 if way == 0 else peers - 1
        holder = lax.rem(place + (peers - step if way == 0 else step), peers)
        block = ring_tile(holder, peers)
        if step == 0:
            src = pert_ref.at[0, :, pl.ds(pl.multiple_of(half + part * piece, LANES), piece)]
        else:
            src = perts_ref.at[block, :, pl.ds(part * piece, piece)]
        number = (way * steps + step) * 2 + part
        return remote(
            src,
            perts_ref.at[block, :, pl.ds(part * piece, piece)],
            ring_send.at[number],
            ring_recv.at[number],
            {"tile": ring_tile(lax.rem(place + towards, peers), peers)},
        )

    def parts_of(way, step):
        if peers % 2 == 0 and step == steps - 1:
            return (way,)
        return (0, 1)

    def ring_step(step):
        for part in (0, 1):
            for way in (0, 1):
                if step > 0 and part in parts_of(way, step - 1):
                    ring_copy(way, step - 1, part).wait_recv()
                if step < steps and part in parts_of(way, step):
                    ring_copy(way, step, part).start()

    if steps > 0:
        ring_step(0)

    def lev_copy(chunk):
        return remote(
            sent_buf.at[chunk], other_buf.at[chunk], lev_send.at[chunk], lev_recv.at[chunk], partner
        )

    rows = bins * group
    weight = jnp.concatenate(split_high_low(weight_ref[...]), axis=0)

    def compute(chunk, carry):
        fetch(chunk).wait()
        here = pl.ds(pl.multiple_of(chunk * width, LANES), width)
        scaled = energy_ref[:, here].astype(jnp.float32) * (
            early_ref[:, here].astype(jnp.float32) + late_ref[:, here].astype(jnp.float32)
        )
        for part in range(members // group):
            those = slice(part * group, (part + 1) * group)
            block = members_buf[chunk, those].astype(jnp.float32) * scaled[None]
            high, low = split_high_low(block.reshape(group * levels, width))
            both = jnp.dot(weight, high, preferred_element_type=jnp.float32)
            summed = both[:rows] + both[rows:]
            summed = summed + jnp.dot(weight[:rows], low, preferred_element_type=jnp.float32)
            shaped = summed.reshape(bins, group, width)
            own_buf[chunk, :, those, :] = shaped
            sent_buf[chunk, :, those, :] = shaped.astype(jnp.bfloat16)
        lev_copy(chunk).start()
        return carry

    lax.fori_loop(0, chunks, compute, 0)
    if steps > 1:
        ring_step(1)

    def finish(chunk):
        here = pl.ds(pl.multiple_of(chunk * width, LANES), width)
        return pltpu.make_async_copy(
            table_buf.at[chunk], summary_ref.at[:, here, :], out_sem.at[chunk]
        )

    def add_other(chunk, carry):
        lev_copy(chunk).wait_recv()
        for bin_id in range(bins):
            for start in range(0, width, LANES):
                here = slice(start, start + LANES)
                summed = own_buf[chunk, bin_id, :, here] + other_buf[chunk, bin_id, :, here].astype(
                    jnp.float32
                )
                padded = jnp.concatenate(
                    [summed, jnp.zeros((LANES - members, LANES), jnp.float32)], axis=0
                )
                table_buf[chunk, bin_id, here, :] = padded.T
        finish(chunk).start()
        return carry

    lax.fori_loop(0, chunks // 2, add_other, 0)
    if steps > 2:
        ring_step(2)
    lax.fori_loop(chunks // 2, chunks, add_other, 0)
    for step in range(3, steps + 1):
        ring_step(step)
    if 1 <= steps <= 2:
        ring_step(steps)
    for way in (0, 1):
        for step in range(steps):
            for part in parts_of(way, step):
                ring_copy(way, step, part).wait_send()
    for copy in look_copies:
        copy.wait()
    own_look.wait()
    own_pert.wait()
    for chunk in range(chunks):
        lev_copy(chunk).wait_send()
        finish(chunk).wait()


def exchange(members_x, error_early, error_late, energy, local_vert, packed, obs_pert, peers, share):
    members, levels, columns = members_x.shape
    bins = local_vert.shape[0]
    group = 16
    width = min(512, columns)
    chunks = columns // width
    ring = max(4 * (peers // 2), 1)
    eye = jnp.eye(group, dtype=jnp.float32)
    weight = (local_vert[:, None, None, :] * eye[None, :, :, None]).reshape(bins * group, group * levels)
    anywhere = pl.BlockSpec(memory_space=pl.ANY)
    near = pl.BlockSpec(memory_space=pltpu.VMEM)
    dma = pltpu.SemaphoreType.DMA
    return pl.pallas_call(
        functools.partial(exchange_kernel, peers, group),
        in_specs=[anywhere, near, near, near, near, near, anywhere],
        out_specs=[anywhere, anywhere, anywhere],
        out_shape=[
            jax.ShapeDtypeStruct((bins, columns, LANES), jnp.float32),
            jax.ShapeDtypeStruct((peers,) + packed.shape, jnp.int32),
            jax.ShapeDtypeStruct((peers, members, share), jnp.bfloat16),
        ],
        scratch_shapes=[
            pltpu.VMEM((chunks, members, levels, width), jnp.bfloat16),
            pltpu.VMEM((chunks, bins, members, width), jnp.float32),
            pltpu.VMEM((chunks, bins, members, width), jnp.bfloat16),
            pltpu.VMEM((chunks, bins, members, width), jnp.bfloat16),
            pltpu.VMEM((chunks, bins, width, LANES), jnp.float32),
            dma((chunks,)),
            dma((chunks,)),
            dma((chunks,)),
            dma((chunks,)),
            dma((max(peers - 1, 1),)),
            dma((max(peers - 1, 1),)),
            dma((ring,)),
            dma((ring,)),
            dma((2,)),
        ],
        compiler_params=pltpu.CompilerParams(
            vmem_limit_bytes=VMEM_LIMIT, collective_id=0, has_side_effects=True
        ),
        name="summary_exchange",
    )(members_x, error_early, error_late, energy, weight, packed, obs_pert)


def dots_kernel(members, summary_ref, lookup_ref, pert_ref, dots_ref, table_ref, rows_ref, table_sem):
    owner = pl.program_id(0)
    peers = pl.num_programs(0)
    tile = lax.axis_index("tile")
    share = pert_ref.shape[2]

    @pl.when(owner == 0)
    def _():
        copy = pltpu.make_async_copy(summary_ref, table_ref, table_sem)
        copy.start()
        copy.wait()

    dots_ref[...] = jnp.zeros_like(dots_ref)
    row_id = lax.broadcasted_iota(jnp.int32, (LANES, LANES), 0)
    col_id = lax.broadcasted_iota(jnp.int32, (LANES, LANES), 1)
    first = lookup_ref[0, 0, share + tile]
    last = lookup_ref[0, 0, share + peers + tile]
    first_chunk = lax.div(first, CHUNK)
    last_chunk = jnp.where(last > first, lax.div(last + CHUNK - 1, CHUNK), first_chunk)

    def gather(chunk):
        base = pl.multiple_of(chunk * CHUNK, CHUNK)
        slot = lax.rem(chunk, 2)
        for place in range(0, CHUNK, 8):
            rows = [
                table_ref[pl.ds(lookup_ref[0, 0, base + place + k], 1), :] for k in range(8)
            ]
            rows_ref[slot, place:place + 8, :] = jnp.concatenate(rows, axis=0)

    def products(chunk):
        base = pl.multiple_of(chunk * CHUNK, CHUNK)
        slot = lax.rem(chunk, 2)
        for sub in range(0, CHUNK, LANES):
            values = rows_ref[slot, sub:sub + LANES, :members]
            high, low = split_high_low(values)
            here = pl.ds(pl.multiple_of(base + sub, LANES), LANES)
            pert = pert_ref[0, :, here]
            product = jnp.dot(high, pert, preferred_element_type=jnp.float32) + jnp.dot(
                low, pert, preferred_element_type=jnp.float32
            )
            picked = jnp.where(row_id == col_id, product, 0.0)
            dots_ref[0, :, here] = jnp.sum(picked, axis=0, keepdims=True)

    def one_chunk(chunk, carry):
        products(chunk - 1)
        gather(chunk)
        return carry

    @pl.when(last_chunk > first_chunk)
    def _():
        gather(first_chunk)
        lax.fori_loop(first_chunk + 1, last_chunk, one_chunk, 0)
        products(last_chunk - 1)


def tile_dots(summary, lookups, perts):
    peers, members, share = perts.shape
    return pl.pallas_call(
        functools.partial(dots_kernel, members),
        grid=(peers,),
        in_specs=[
            pl.BlockSpec(memory_space=pl.ANY),
            pl.BlockSpec((1, 1, lookups.shape[2]), lambda i: (i, 0, 0), memory_space=pltpu.SMEM),
            pl.BlockSpec((1, members, share), lambda i: (i, 0, 0)),
        ],
        out_specs=pl.BlockSpec((1, 1, share), lambda i: (i, 0, 0)),
        out_shape=jax.ShapeDtypeStruct((peers, 1, share), jnp.float32),
        scratch_shapes=[
            pltpu.VMEM(summary.shape, jnp.float32),
            pltpu.VMEM((2, CHUNK, LANES), jnp.float32),
            pltpu.SemaphoreType.DMA,
        ],
        compiler_params=pltpu.CompilerParams(vmem_limit_bytes=VMEM_LIMIT),
        name="tile_dots",
    )(summary, lookups, perts)


def combine_kernel(
    peers,
    members,
    dots_ref,
    lists_ref,
    block_ref,
    innovation_ref,
    variance_ref,
    horiz_ref,
    out_ref,
    landed,
    halves,
    send_sem,
    recv_sem,
    lev_send,
    lev_recv,
):
    tile = lax.axis_index("tile")
    lev = lax.axis_index("lev")
    share = dots_ref.shape[2]
    blocks, later_slots = lists_ref.shape[1], lists_ref.shape[2]
    greet(peers, tile, lev)
    copies = []
    for offset in range(1, peers):
        target = lax.rem(tile + offset, peers)
        copy = remote(
            dots_ref.at[target],
            landed.at[tile],
            send_sem.at[offset - 1],
            recv_sem.at[offset - 1],
            {"tile": target},
        )
        copy.start()
        copies.append(copy)
    here = pl.ds(pl.multiple_of(lev * share, LANES), share)
    block = block_ref[:, here]
    listed = []
    for entry in range(later_slots):
        peer = jnp.zeros(block.shape, jnp.int32)
        for number in range(blocks):
            peer = jnp.where(block == number, lists_ref[0, number, entry], peer)
        listed.append(peer)
    weights = [horiz_ref[0, entry:entry + 1, here] for entry in range(later_slots + 1)]
    scale = innovation_ref[:, here] * variance_ref[:, here] / (members - 1.0)
    total = weights[0] * dots_ref[tile]
    for offset in range(1, peers):
        copies[offset - 1].wait_recv()
        sender = lax.rem(tile + peers - offset, peers)
        weight = jnp.zeros(total.shape, jnp.float32)
        for entry in range(later_slots):
            weight = weight + jnp.where(listed[entry] == sender, weights[entry + 1], 0.0)
        total = total + weight * landed[sender]
    impact = scale * total
    rows = share // LANES
    for row in range(rows):
        halves[lev, row % 2, row // 2:row // 2 + 1, :] = impact[:, row * LANES:(row + 1) * LANES]
    swap = remote(halves.at[lev], halves.at[lev], lev_send, lev_recv, {"lev": 1 - lev})
    swap.start()
    from_id = lax.broadcasted_iota(jnp.int32, (LANES, LANES), 0)
    to_id = lax.broadcasted_iota(jnp.int32, (LANES, LANES), 1)
    wanted = 2 * to_id + lev
    even = jnp.where(from_id == wanted, 1.0, 0.0)
    odd = jnp.where(from_id == wanted - LANES, 1.0, 0.0)
    swap.wait()
    for place in range(2):
        out_ref[place] = jnp.dot(
            halves[place, 0], even, precision=lax.Precision.HIGHEST, preferred_element_type=jnp.float32
        ) + jnp.dot(
            halves[place, 1], odd, precision=lax.Precision.HIGHEST, preferred_element_type=jnp.float32
        )
    for copy in copies:
        copy.wait_send()


def combine(dots, tile_lists, obs_block, innovation, inv_variance, horiz_weight, members):
    peers, _, share = dots.shape
    rows = share // LANES
    near = pl.BlockSpec(memory_space=pltpu.VMEM)
    dma = pltpu.SemaphoreType.DMA
    return pl.pallas_call(
        functools.partial(combine_kernel, peers, members),
        in_specs=[near, pl.BlockSpec(memory_space=pltpu.SMEM), near, near, near, near],
        out_specs=near,
        out_shape=jax.ShapeDtypeStruct((2, rows // 2, LANES), jnp.float32),
        scratch_shapes=[
            pltpu.VMEM((peers, 1, share), jnp.float32),
            pltpu.VMEM((2, 2, rows // 2, LANES), jnp.float32),
            dma((max(peers - 1, 1),)),
            dma((max(peers - 1, 1),)),
            dma,
            dma,
        ],
        compiler_params=pltpu.CompilerParams(
            vmem_limit_bytes=VMEM_LIMIT, collective_id=1, has_side_effects=True
        ),
        name="combine_dots",
    )(dots, tile_lists, obs_block, innovation, inv_variance, horiz_weight)


def on_device(
    members_x,
    error_early,
    error_late,
    energy,
    vert_weight,
    tile_lists,
    obs_block,
    obs_bin,
    obs_column,
    obs_pert,
    innovation,
    inv_variance,
    horiz_weight,
):
    lev_count = lax.axis_size("lev")
    lev_place = lax.axis_index("lev")
    peers = lax.axis_size("tile")
    tile_place = lax.axis_index("tile")
    members = members_x.shape[0]
    levels_here = members_x.shape[1]
    columns = members_x.shape[2]
    tile_table = tile_lists[0]
    blocks = tile_table.shape[0]
    later_slots = tile_table.shape[1]
    obs_count = obs_block.shape[1]
    share = obs_count // lev_count

    half = lev_place * share
    lookup = obs_bin[0] * columns + obs_column[0]
    lookup_half = lax.dynamic_slice_in_dim(lookup, half, share, 0)

    tile_ids = jnp.arange(peers, dtype=jnp.int32)
    block_ids = jnp.arange(blocks, dtype=jnp.int32)
    starts = jnp.sum((obs_block[0][None, :] < block_ids[:, None]).astype(jnp.int32), axis=1)
    ends = jnp.sum((obs_block[0][None, :] <= block_ids[:, None]).astype(jnp.int32), axis=1)
    listed = jnp.any(tile_table[:, :, None] == tile_ids[None, None, :], axis=1)
    range_first = jnp.sum(jnp.where(listed, starts[:, None], 0), axis=0)
    range_last = jnp.sum(jnp.where(listed, ends[:, None], 0), axis=0)
    range_first = jnp.where(tile_ids == tile_place, 0, range_first)
    range_last = jnp.where(tile_ids == tile_place, obs_count, range_last)
    range_first = jnp.clip(range_first - half, 0, share)
    range_last = jnp.clip(range_last - half, 0, share)
    spare = jnp.zeros(((-2 * peers) % LANES,), jnp.int32)
    packed = jnp.concatenate([lookup_half, range_first, range_last, spare])[None, :]

    local_vert = lax.dynamic_slice_in_dim(vert_weight, lev_place * levels_here, levels_here, 1)
    summary, everyone, perts = exchange(
        members_x, error_early, error_late, energy, local_vert, packed, obs_pert, peers, share
    )
    table = summary.reshape(-1, LANES)
    dots = tile_dots(table, everyone, perts)
    impact = combine(dots, tile_lists, obs_block, innovation, inv_variance, horiz_weight, members)
    return impact.reshape(1, obs_count // lev_count, 1)


def solution(mesh):
    return jax.shard_map(
        on_device,
        mesh=mesh,
        in_specs=(
            P(None, "lev", ("group", "tile")),
            P("lev", ("group", "tile")),
            P("lev", ("group", "tile")),
            P("lev", ("group", "tile")),
            P(),
            P(("group", "tile"), None, None),
            P(("group", "tile"), None),
            P(("group", "tile"), None),
            P(("group", "tile"), None),
            P(("group", "tile"), None, None),
            P(("group", "tile"), None),
            P(("group", "tile"), None),
            P(("group", "tile"), None, None),
        ),
        out_specs=P(("group", "tile"), None, "lev"),
        check_vma=False,
    )
```

profile of v0, /device:TPU:5, one launch (start us, length us, event | category | flops | bytes accessed | tf_op | source)
XLA Modules:
  0.0 69.9 jit_solution(6919234910420446145)
XLA Ops:
  0.0 0.0 copy-start
  0.0 0.8 %fusion.3 = pred[2,8]{1,0:T(4,128)(4,1)S(1)} fusion(s32[2,3]{1,0:T(2,128)} %bitcast.11), kind=kLoop, calls=%fused_computation.10 | loop fusion | flops 80 | bytes 40 | tf_op jit(solution)/shard_map/reduce_or | solution.py:487
  0.8 0.9 %fusion.1 = (s32[2]{0:T(128)S(1)}, s32[2]{0:T(128)S(1)}) fusion(s32[4096]{0:T(1024)} %bitcast.8), kind=kLoop, calls=%fused_computation.4 | loop fusion | flops 49148 | bytes 16400 | tf_op jit(solution)/shard_map/reduce_sum | solution.py:486
  1.7 0.1 select_reduce_fusion
  1.8 0.0 copy-done
  1.8 0.1 constant_dynamic-slice_fusion
  1.9 0.7 %dynamic-slice_add_fusion = s32[1,2048]{1,0:T(1,128)S(1)} fusion(s32[1,4096]{1,0:T(1,128)} %param.21, s32[]{:T(128)S(6)} %select_n.21, s32[1,4096]{1,0:T(1,128)} %param.20), kind=kLoop, calls=%fused_computation.5 | loop fusion | flops 4096 | bytes 24580 | tf_op jit(solution)/shard_map/add | solution.py:480
  2.6 0.1 concatenate.3
  2.7 0.6 broadcast_in_dim.41.packed_ref
  3.3 0.2 broadcast_multiply_fusion
  3.5 1.1 %mul.34.weight_ref = f32[128,256]{1,0:T(8,128)} reshape(f32[8,16,16,16]{3,2,1,0:T(8,128)S(1)} %broadcast_multiply_fusion) | data formatting | bytes 262144 | tf_op jit(solution)/shard_map/mul | solution.py:239
  4.5 32.8 %summary_exchange.1 = (f32[8,2048,128]{2,1,0:T(8,128)}, s32[8,1,2176]{2,1,0:T(1,128)}, bf16[8,80,2048]{2,1,0:T(8,128)(2,1)}) custom-call(bf16[80,16,2048]{2,1,0:T(8,128)(2,1)} %members_ref.1, bf16[16,2048]{1,0:T(8,128)(2,1)} %early_ref.1, bf16[16,2048]{1,0:T(8,128)(2,1)} %late_ref.1, bf16[16,2048]{1,0:T(8,128)(2,1)} %energy_ref.1, ...), custom_call_target="tpu_custom_call" | custom-call | tf_op jit(solution)/shard_map/summary_exchange/pallas_call | solution.py:243
  37.3 16.4 %tile_dots.1.dots_ref = f32[8,1,2048]{2,1,0:T(1,128)} custom-call(f32[16384,128]{1,0:T(8,128)} %bitcast.7, s32[8,1,2176]{2,1,0:T(1,128)} %get-tuple-element.9.lookup_ref, bf16[8,80,2048]{2,1,0:T(8,128)(2,1)} %get-tuple-element.10.pert_ref), custom_call_target="tpu_custom_call" | custom-call | tf_op jit(solution)/shard_map/tile_dots/pallas_call | solution.py:332
  53.7 14.9 %combine_dots.1 = f32[2,8,128]{2,1,0:T(8,128)} custom-call(f32[8,1,2048]{2,1,0:T(1,128)} %tile_dots.1.dots_ref, s32[1,2,3]{2,1,0:T(2,128)} %lists_ref.1, s32[1,4096]{1,0:T(1,128)} %block_ref.1, f32[1,4096]{1,0:T(1,128)} %innovation_ref.1, f32[1,4096]{1,0:T(1,128)} %variance_ref.1, f32[1,4,4096]{2,1,0:T(4,128)} %horiz_ref.1), custom_call_target="tpu_custom_call" | custom-call | tf_op jit(solution)/shard_map/combine_dots/pallas_call | solution.py:431
  68.6 1.3 %copy.15 = f32[1,2048,1]{1,2,0:T(1,128)} copy(f32[1,2048,1]{1,2,0:T(1,128)} %bitcast.9) | data formatting | bytes 16384
  (3 shorter events, 0.0 us)
Async XLA Ops:
  0.0 1.8 %copy-start = (f32[8,32]{1,0:T(8,128)S(1)}, f32[8,32]{1,0:T(8,128)}, u32[]{:S(2)}) copy-start(f32[8,32]{1,0:T(8,128)} %param.17) | copy-start | bytes 3076
where the time goes:
time: 69.6 us; the launch traced here: 69.9 us
  Pallas kernels  64 us (92%)
  local copies, waits for them, and re-layouts  3.12 us (4%)
  other arithmetic  2.66 us (4%)
    pallas_call x1, Pallas kernels, exchange(): pl.pallas_call(functools.partial(exchange_kernel, peers, group), in_specs...  32.8 us
    pallas_call x1, Pallas kernels, tile_dots(): pl.pallas_call(functools.partial(dots_kernel, members), grid=(peers,), in...  16.4 us
    pallas_call x1, Pallas kernels, combine(): pl.pallas_call(functools.partial(combine_kernel, peers, members), in_spec...  14.9 us

commit v1 on v0

--- a/solution.py
+++ b/solution.py
@@ -54,6 +54,44 @@
         barrier, inc=1, device_id={"lev": 1 - lev}, device_id_type=pl.DeviceIdType.MESH
     )
     pl.semaphore_wait(barrier, peers)
+
+
+def gather_rows(table_ref, lookup_ref, which, rows_ref, chunk):
+    base = pl.multiple_of(chunk * CHUNK, CHUNK)
+    slot = lax.rem(chunk, 2)
+    for place in range(0, CHUNK, 8):
+        rows = [
+            table_ref[pl.ds(lookup_ref[which, 0, base + place + k], 1), :] for k in range(8)
+        ]
+        rows_ref[slot, place:place + 8, :] = jnp.concatenate(rows, axis=0)
+
+
+def dot_rows(rows_ref, pert_ref, dots_ref, which, chunk):
+    members = pert_ref.shape[1]
+    base = pl.multiple_of(chunk * CHUNK, CHUNK)
+    slot = lax.rem(chunk, 2)
+    row_id = lax.broadcasted_iota(jnp.int32, (LANES, LANES), 0)
+    col_id = lax.broadcasted_iota(jnp.int32, (LANES, LANES), 1)
+    for sub in range(0, CHUNK, LANES):
+        high, low = split_high_low(rows_ref[slot, sub:sub + LANES, :members])
+        here = pl.ds(pl.multiple_of(base + sub, LANES), LANES)
+        pert = pert_ref[which, :, here]
+        product = jnp.dot(high, pert, preferred_element_type=jnp.float32) + jnp.dot(
+            low, pert, preferred_element_type=jnp.float32
+        )
+        picked = jnp.where(row_id == col_id, product, 0.0)
+        dots_ref[which, :, here] = jnp.sum(picked, axis=0, keepdims=True)
+
+
+def dots_of_chunks(table_ref, lookup_ref, rows_ref, pert_ref, dots_ref, which, first, last):
+    def one_chunk(chunk, carry):
+        dot_rows(rows_ref, pert_ref, dots_ref, which, chunk - 1)
+        gather_rows(table_ref, lookup_ref, which, rows_ref, chunk)
+        return carry
+
+    gather_rows(table_ref, lookup_ref, which, rows_ref, first)
+    lax.fori_loop(first + 1, last, one_chunk, 0)
+    dot_rows(rows_ref, pert_ref, dots_ref, which, last - 1)
 
 
 def exchange_kernel(
@@ -69,11 +107,15 @@
     summary_ref,
     lookups_ref,
     perts_ref,
+    early_ref_out,
     members_buf,
     own_buf,
     sent_buf,
     other_buf,
     table_buf,
+    look_buf,
+    pert_buf,
+    rows_buf,
     in_sem,
     out_sem,
     lev_send,
@@ -83,6 +125,7 @@
     ring_send,
     ring_recv,
     local_sem,
+    early_sem,
 ):
     tile = lax.axis_index("tile")
     lev = lax.axis_index("lev")
@@ -106,6 +149,12 @@
         pert_ref.at[0, :, pl.ds(half, share)], perts_ref.at[tile], local_sem.at[1]
     )
     own_pert.start()
+    early_copies = [
+        pltpu.make_async_copy(packed_ref, look_buf.at[0], early_sem.at[0]),
+        pltpu.make_async_copy(pert_ref.at[0, :, pl.ds(half, share)], pert_buf.at[0], early_sem.at[1]),
+    ]
+    for copy in early_copies:
+        copy.start()
     greet(peers, tile, lev)
 
     look_copies = []
@@ -186,11 +235,17 @@
     if steps > 1:
         ring_step(1)
 
-    def finish(chunk):
-        here = pl.ds(pl.multiple_of(chunk * width, LANES), width)
-        return pltpu.make_async_copy(
-            table_buf.at[chunk], summary_ref.at[:, here, :], out_sem.at[chunk]
-        )
+    for copy in look_copies:
+        copy.wait_recv()
+    neighbours = (lax.rem(place + peers - 1, peers), lax.rem(place + 1, peers)) if steps > 1 else ()
+    for number, neighbour in enumerate(neighbours, 1):
+        block = ring_tile(neighbour, peers)
+        early_copies += [
+            pltpu.make_async_copy(lookups_ref.at[block], look_buf.at[number], early_sem.at[2 * number]),
+            pltpu.make_async_copy(perts_ref.at[block], pert_buf.at[number], early_sem.at[2 * number + 1]),
+        ]
+    for copy in early_copies[2:]:
+        copy.start()
 
     def add_other(chunk, carry):
         lev_copy(chunk).wait_recv()
@@ -203,15 +258,30 @@
                 padded = jnp.concatenate(
                     [summed, jnp.zeros((LANES - members, LANES), jnp.float32)], axis=0
                 )
-                table_buf[chunk, bin_id, here, :] = padded.T
-        finish(chunk).start()
+                row = pl.multiple_of(bin_id * chunks * width + chunk * width + start, LANES)
+                table_buf[pl.ds(row, LANES), :] = padded.T
         return carry
 
     lax.fori_loop(0, chunks // 2, add_other, 0)
     if steps > 2:
         ring_step(2)
     lax.fori_loop(chunks // 2, chunks, add_other, 0)
-    for step in range(3, steps + 1):
+    table_out = pltpu.make_async_copy(table_buf, summary_ref, out_sem)
+    table_out.start()
+
+    def early_dots(number):
+        for copy in early_copies[2 * number:2 * number + 2]:
+            copy.wait()
+        dots_of_chunks(
+            table_buf, look_buf, rows_buf, pert_buf, early_ref_out, number, 0, share // CHUNK
+        )
+
+    early_dots(0)
+    if steps > 3:
+        ring_step(3)
+    for number in range(1, len(neighbours) + 1):
+        early_dots(number)
+    for step in range(4 if steps > 3 else 3, steps + 1):
         ring_step(step)
     if 1 <= steps <= 2:
         ring_step(steps)
@@ -220,12 +290,12 @@
             for part in parts_of(way, step):
                 ring_copy(way, step, part).wait_send()
     for copy in look_copies:
-        copy.wait()
+        copy.wait_send()
     own_look.wait()
     own_pert.wait()
     for chunk in range(chunks):
         lev_copy(chunk).wait_send()
-        finish(chunk).wait()
+    table_out.wait()
 
 
 def exchange(members_x, error_early, error_late, energy, local_vert, packed, obs_pert, peers, share):
@@ -242,21 +312,25 @@
     dma = pltpu.SemaphoreType.DMA
     return pl.pallas_call(
         functools.partial(exchange_kernel, peers, group),
-        in_specs=[anywhere, near, near, near, near, near, anywhere],
-        out_specs=[anywhere, anywhere, anywhere],
+        in_specs=[anywhere, near, near, near, near, anywhere, anywhere],
+        out_specs=[anywhere, anywhere, anywhere, near],
         out_shape=[
-            jax.ShapeDtypeStruct((bins, columns, LANES), jnp.float32),
+            jax.ShapeDtypeStruct((bins * columns, LANES), jnp.float32),
             jax.ShapeDtypeStruct((peers,) + packed.shape, jnp.int32),
             jax.ShapeDtypeStruct((peers, members, share), jnp.bfloat16),
+            jax.ShapeDtypeStruct((3, 1, share), jnp.float32),
         ],
         scratch_shapes=[
             pltpu.VMEM((chunks, members, levels, width), jnp.bfloat16),
             pltpu.VMEM((chunks, bins, members, width), jnp.float32),
             pltpu.VMEM((chunks, bins, members, width), jnp.bfloat16),
             pltpu.VMEM((chunks, bins, members, width), jnp.bfloat16),
-            pltpu.VMEM((chunks, bins, width, LANES), jnp.float32),
+            pltpu.VMEM((bins * columns, LANES), jnp.float32),
+            pltpu.SMEM((3,) + packed.shape, jnp.int32),
+            pltpu.VMEM((3, members, share), jnp.bfloat16),
+            pltpu.VMEM((2, CHUNK, LANES), jnp.float32),
             dma((chunks,)),
-            dma((chunks,)),
+            dma,
             dma((chunks,)),
             dma((chunks,)),
             dma((max(peers - 1, 1),)),
@@ -264,6 +338,7 @@
             dma((ring,)),
             dma((ring,)),
             dma((2,)),
+            dma((6,)),
         ],
         compiler_params=pltpu.CompilerParams(
             vmem_limit_bytes=VMEM_LIMIT, collective_id=0, has_side_effects=True
@@ -272,9 +347,10 @@
     )(members_x, error_early, error_late, energy, weight, packed, obs_pert)
 
 
-def dots_kernel(members, summary_ref, lookup_ref, pert_ref, dots_ref, table_ref, rows_ref, table_sem):
+def dots_kernel(
+    peers, summary_ref, lookup_ref, pert_ref, early_ref, dots_ref, table_ref, rows_ref, table_sem
+):
     owner = pl.program_id(0)
-    peers = pl.num_programs(0)
     tile = lax.axis_index("tile")
     share = pert_ref.shape[2]
 
@@ -284,58 +360,43 @@
         copy.start()
         copy.wait()
 
-    dots_ref[...] = jnp.zeros_like(dots_ref)
-    row_id = lax.broadcasted_iota(jnp.int32, (LANES, LANES), 0)
-    col_id = lax.broadcasted_iota(jnp.int32, (LANES, LANES), 1)
-    first = lookup_ref[0, 0, share + tile]
-    last = lookup_ref[0, 0, share + peers + tile]
-    first_chunk = lax.div(first, CHUNK)
-    last_chunk = jnp.where(last > first, lax.div(last + CHUNK - 1, CHUNK), first_chunk)
-
-    def gather(chunk):
-        base = pl.multiple_of(chunk * CHUNK, CHUNK)
-        slot = lax.rem(chunk, 2)
-        for place in range(0, CHUNK, 8):
-            rows = [
-                table_ref[pl.ds(lookup_ref[0, 0, base + place + k], 1), :] for k in range(8)
-            ]
-            rows_ref[slot, place:place + 8, :] = jnp.concatenate(rows, axis=0)
-
-    def products(chunk):
-        base = pl.multiple_of(chunk * CHUNK, CHUNK)
-        slot = lax.rem(chunk, 2)
-        for sub in range(0, CHUNK, LANES):
-            values = rows_ref[slot, sub:sub + LANES, :members]
-            high, low = split_high_low(values)
-            here = pl.ds(pl.multiple_of(base + sub, LANES), LANES)
-            pert = pert_ref[0, :, here]
-            product = jnp.dot(high, pert, preferred_element_type=jnp.float32) + jnp.dot(
-                low, pert, preferred_element_type=jnp.float32
+    apart = lax.rem(ring_place(owner, peers) - ring_place(tile, peers) + peers, peers)
+    ready = (apart == 0) | (((apart == 1) | (apart == peers - 1)) & (peers > 3))
+
+    @pl.when(ready)
+    def _():
+        dots_ref[0] = early_ref[jnp.where(apart == 0, 0, jnp.where(apart == 1, 2, 1))]
+
+    @pl.when(jnp.logical_not(ready))
+    def _():
+        dots_ref[...] = jnp.zeros_like(dots_ref)
+        first = lookup_ref[0, 0, share + tile]
+        last = lookup_ref[0, 0, share + peers + tile]
+
+        @pl.when(last > first)
+        def _():
+            dots_of_chunks(
+                table_ref,
+                lookup_ref,
+                rows_ref,
+                pert_ref,
+                dots_ref,
+                0,
+                lax.div(first, CHUNK),
+                lax.div(last + CHUNK - 1, CHUNK),
             )
-            picked = jnp.where(row_id == col_id, product, 0.0)
-            dots_ref[0, :, here] = jnp.sum(picked, axis=0, keepdims=True)
-
-    def one_chunk(chunk, carry):
-        products(chunk - 1)
-        gather(chunk)
-        return carry
-
-    @pl.when(last_chunk > first_chunk)
-    def _():
-        gather(first_chunk)
-        lax.fori_loop(first_chunk + 1, last_chunk, one_chunk, 0)
-        products(last_chunk - 1)
-
-
-def tile_dots(summary, lookups, perts):
+
+
+def tile_dots(summary, lookups, perts, early):
     peers, members, share = perts.shape
     return pl.pallas_call(
-        functools.partial(dots_kernel, members),
+        functools.partial(dots_kernel, peers),
         grid=(peers,),
         in_specs=[
             pl.BlockSpec(memory_space=pl.ANY),
             pl.BlockSpec((1, 1, lookups.shape[2]), lambda i: (i, 0, 0), memory_space=pltpu.SMEM),
             pl.BlockSpec((1, members, share), lambda i: (i, 0, 0)),
+            pl.BlockSpec(early.shape, lambda i: (0, 0, 0)),
         ],
         out_specs=pl.BlockSpec((1, 1, share), lambda i: (i, 0, 0)),
         out_shape=jax.ShapeDtypeStruct((peers, 1, share), jnp.float32),
@@ -346,7 +407,7 @@
         ],
         compiler_params=pltpu.CompilerParams(vmem_limit_bytes=VMEM_LIMIT),
         name="tile_dots",
-    )(summary, lookups, perts)
+    )(summary, lookups, perts, early)
 
 
 def combine_kernel(
@@ -495,11 +556,10 @@
     packed = jnp.concatenate([lookup_half, range_first, range_last, spare])[None, :]
 
     local_vert = lax.dynamic_slice_in_dim(vert_weight, lev_place * levels_here, levels_here, 1)
-    summary, everyone, perts = exchange(
+    summary, everyone, perts, early = exchange(
         members_x, error_early, error_late, energy, local_vert, packed, obs_pert, peers, share
     )
-    table = summary.reshape(-1, LANES)
-    dots = tile_dots(table, everyone, perts)
+    dots = tile_dots(summary, everyone, perts, early)
     impact = combine(dots, tile_lists, obs_block, innovation, inv_variance, horiz_weight, members)
     return impact.reshape(1, obs_count // lev_count, 1)
 

time: 69.6 us -> 71.3 us (1.024)
  the two profiles are of different devices: /device:TPU:5 before, /device:TPU:0 now
where the time goes in v1:
time: 71.3 us; the launch traced here: 70.7 us
  Pallas kernels  64.8 us (91%)
  local copies, waits for them, and re-layouts  3.12 us (4%)
  other arithmetic  2.66 us (4%)
    pallas_call x1, Pallas kernels, exchange(): pl.pallas_call(functools.partial(exchange_kernel, peers, group), in_specs...  40.7 us
    pallas_call x1, Pallas kernels, tile_dots(): pl.pallas_call(functools.partial(dots_kernel, peers), grid=(peers,), in_s...  12.5 us
    pallas_call x1, Pallas kernels, combine(): pl.pallas_call(functools.partial(combine_kernel, peers, members), in_spec...  11.7 us

profile of v1, /device:TPU:0, one launch (start us, length us, event | category | flops | bytes accessed | tf_op | source)
XLA Modules:
  0.0 70.7 jit_solution(5471628147220032735)
XLA Ops:
  0.0 0.0 copy-start
  0.0 0.8 %fusion.3 = pred[2,8]{1,0:T(4,128)(4,1)S(1)} fusion(s32[2,3]{1,0:T(2,128)} %bitcast.9), kind=kLoop, calls=%fused_computation.10 | loop fusion | flops 80 | bytes 40 | tf_op jit(solution)/shard_map/reduce_or | solution.py:548
  0.8 0.9 %fusion.1 = (s32[2]{0:T(128)S(1)}, s32[2]{0:T(128)S(1)}) fusion(s32[4096]{0:T(1024)} %bitcast.6), kind=kLoop, calls=%fused_computation.4 | loop fusion | flops 49148 | bytes 16400 | tf_op jit(solution)/shard_map/reduce_sum | solution.py:547
  1.7 0.1 select_reduce_fusion
  1.8 0.0 copy-done
  1.8 0.1 constant_dynamic-slice_fusion
  1.9 0.7 %dynamic-slice_add_fusion = s32[1,2048]{1,0:T(1,128)S(1)} fusion(s32[1,4096]{1,0:T(1,128)} %param.21, s32[]{:T(128)S(6)} %select_n.21, s32[1,4096]{1,0:T(1,128)} %param.20), kind=kLoop, calls=%fused_computation.5 | loop fusion | flops 4096 | bytes 24580 | tf_op jit(solution)/shard_map/add | solution.py:541
  2.6 0.1 concatenate.3
  2.7 0.6 broadcast_in_dim.41.packed_ref
  3.3 0.2 broadcast_multiply_fusion
  3.5 1.1 %mul.34.weight_ref = f32[128,256]{1,0:T(8,128)} reshape(f32[8,16,16,16]{3,2,1,0:T(8,128)S(1)} %broadcast_multiply_fusion) | data formatting | bytes 262144 | tf_op jit(solution)/shard_map/mul | solution.py:309
  4.5 40.7 %summary_exchange.1 = (f32[16384,128]{1,0:T(8,128)}, s32[8,1,2176]{2,1,0:T(1,128)}, bf16[8,80,2048]{2,1,0:T(8,128)(2,1)}, f32[3,1,2048]{2,1,0:T(1,128)}) custom-call(bf16[80,16,2048]{2,1,0:T(8,128)(2,1)} %members_ref.1, bf16[16,2048]{1,0:T(8,128)(2,1)} %early_ref.1, bf16[16,2048]{1,0:T(8,128)(2,1)} %late_ref.1, bf16[16,2048]{1,0:T(8,128)(2,1)} %energy_ref.1, ...), custom_call_target="tpu_custom_call" | custom-call | tf_op jit(solution)/shard_map/summary_exchange/pallas_call | solution.py:313
  45.2 12.5 %tile_dots.1.dots_ref = f32[8,1,2048]{2,1,0:T(1,128)} custom-call(f32[16384,128]{1,0:T(8,128)} %get-tuple-element.9.summary_ref, s32[8,1,2176]{2,1,0:T(1,128)} %get-tuple-element.10.lookup_ref, bf16[8,80,2048]{2,1,0:T(8,128)(2,1)} %get-tuple-element.11.pert_ref, f32[3,1,2048]{2,1,0:T(1,128)} %get-tuple-element.12.early_ref), custom_call_target="tpu_custom_call" | custom-call | tf_op jit(solution)/shard_map/tile_dots/pallas_call | solution.py:392
  57.7 11.7 %combine_dots.1 = f32[2,8,128]{2,1,0:T(8,128)} custom-call(f32[8,1,2048]{2,1,0:T(1,128)} %tile_dots.1.dots_ref, s32[1,2,3]{2,1,0:T(2,128)} %lists_ref.1, s32[1,4096]{1,0:T(1,128)} %block_ref.1, f32[1,4096]{1,0:T(1,128)} %innovation_ref.1, f32[1,4096]{1,0:T(1,128)} %variance_ref.1, f32[1,4,4096]{2,1,0:T(4,128)} %horiz_ref.1), custom_call_target="tpu_custom_call" | custom-call | tf_op jit(solution)/shard_map/combine_dots/pallas_call | solution.py:492
  69.4 1.3 %copy.15 = f32[1,2048,1]{1,2,0:T(1,128)} copy(f32[1,2048,1]{1,2,0:T(1,128)} %bitcast.7) | data formatting | bytes 16384
  (3 shorter events, 0.0 us)
Async XLA Ops:
  0.0 1.8 %copy-start = (f32[8,32]{1,0:T(8,128)S(1)}, f32[8,32]{1,0:T(8,128)}, u32[]{:S(2)}) copy-start(f32[8,32]{1,0:T(8,128)} %param.17) | copy-start | bytes 3076
